TPU v7x, 32 devices: a whole 2x2x4 slice. The times are simulated.
32 devices in a mesh: col: 4 (over z), dp: 8 (over y, x, core).
Axes of the slice: x: 2, y: 2, z: 4, core: 2. Of those that a mesh axis runs over, the one named last changes fastest.
Arguments:
- tokens: bfloat16 [512, 8192], P('col', 'dp'), may hold values from -6 to 6
- cotangent: bfloat16 [512, 8192], P('col', 'dp'), may hold values from -0.1796875 to 0.1796875
- gate_weight: bfloat16 [8192, 14336], P('dp', 'col'), may hold values from -0.09375 to 0.09375
- up_weight: bfloat16 [8192, 14336], P('dp', 'col'), may hold values from -0.09375 to 0.09375
- down_weight: bfloat16 [14336, 8192], P('col', 'dp'), may hold values from -0.0625 to 0.0625
- gate_mask: int32 [64, 112], P('dp', 'col'), may hold values 0 or 1
- up_mask: int32 [64, 112], P('dp', 'col'), may hold values 0 or 1
- down_mask: int32 [112, 64], P('col', 'dp'), may hold values 0 or 1
- counts: int32 [4], P('col'), may hold values from 1 to 128, 384 in all
Outputs:
- output: bfloat16 [512, 8192], P('col', 'dp')
- gate_grad: float32 [8192, 14336], P('dp', 'col')
- up_grad: float32 [8192, 14336], P('dp', 'col')
- down_grad: float32 [14336, 8192], P('col', 'dp')
Inputs may be any that keep to these rules, and one draw needn't show every extreme that they name: `counts`: the largest count equals 128.
All inputs are finite; a program needn't handle non-finite values. No bound on the sum of `gate_mask` or of `up_mask` or of `down_mask` or of `counts` on one device may be relied on, other than what follows from the above.
Results may differ from a plain program's by a relative error of at most 0.039.
Values may be sent and summed in bfloat16 or wider, within the bound.
A program may use at most 192 MiB of HBM per device.

v0:
```python
import jax
import jax.numpy as jnp
from jax import lax
from jax.sharding import PartitionSpec as P


def widen(mask, weight):
    rows, cols = mask.shape
    height = weight.shape[0] // rows
    breadth = weight.shape[1] // cols
    shaped = weight.reshape(rows, height, cols, breadth)
    keep = (mask > 0)[:, None, :, None]
    return jnp.where(keep, shaped, jnp.zeros_like(shaped)).reshape(weight.shape)


def activate(gate_up, units):
    gate = gate_up[:, :units]
    upward = gate_up[:, units:]
    sigma = jax.nn.sigmoid(gate)
    active = gate * sigma
    hidden = (active * upward).astype(jnp.bfloat16)
    return (gate, upward, sigma, active, hidden)


def derive(gate, upward, sigma, active, back):
    d_gate = (back * upward * sigma * (1.0 + gate * (1.0 - sigma))).astype(jnp.bfloat16)
    d_up = (back * active).astype(jnp.bfloat16)
    return jnp.concatenate([d_gate, d_up], axis=1)


def on_device(
    tokens, cotangent, gate_weight, up_weight, down_weight, gate_mask, up_mask, down_mask, counts
):
    tok_dev = tokens.shape[0]
    live = (lax.iota(jnp.int32, tok_dev) < counts[0])[:, None]
    g_live = jnp.where(live, cotangent, jnp.zeros_like(cotangent))
    tok_all, grad_all = (
        lax.all_gather(tokens, "col", axis=0, tiled=True),
        lax.all_gather(g_live, "col", axis=0, tiled=True),
    )
    w_gate = widen(gate_mask, gate_weight)
    w_up = widen(up_mask, up_weight)
    w_down = widen(down_mask, down_weight)
    w_both = jnp.concatenate([w_gate, w_up], axis=1)
    units = gate_weight.shape[1]
    contract_rows = (((0,), (0,)), ((), ()))
    contract_cols = (((1,), (1,)), ((), ()))
    block = tok_all
    gate_up = lax.psum_scatter(
        jnp.dot(block, w_both, preferred_element_type=jnp.float32).astype(jnp.bfloat16),
        "dp",
        scatter_dimension=0,
        tiled=True,
    ).astype(jnp.float32)
    gate, upward, sigma, active, hidden_mine = activate(gate_up, units)
    hidden_all = lax.all_gather(hidden_mine, "dp", axis=0, tiled=True)
    block = grad_all
    back = lax.psum_scatter(
        lax.dot_general(block, w_down, contract_cols, preferred_element_type=jnp.float32).astype(
            jnp.bfloat16
        ),
        "dp",
        scatter_dimension=0,
        tiled=True,
    ).astype(jnp.float32)
    d_mine = derive(gate, upward, sigma, active, back)
    block = tok_all
    grads = lax.dot_general(
        block,
        lax.all_gather(d_mine, "dp", axis=0, tiled=True),
        contract_rows,
        preferred_element_type=jnp.float32,
    )
    block = hidden_all
    mixed = lax.psum_scatter(
        jnp.dot(block, w_down, preferred_element_type=jnp.float32).astype(jnp.bfloat16),
        "col",
        scatter_dimension=0,
        tiled=True,
    ).astype(jnp.float32)
    output = jnp.where(live, mixed, jnp.zeros_like(mixed)).astype(jnp.bfloat16)
    down_full = lax.dot_general(
        hidden_all, grad_all, contract_rows, preferred_element_type=jnp.float32
    )
    gate_grad = widen(gate_mask, grads[:, :units])
    up_grad = widen(up_mask, grads[:, units:])
    down_grad = widen(down_mask, down_full)
    return (output, gate_grad, up_grad, down_grad)


def solution(mesh):
    in_specs = (
        P("col", "dp"),
        P("col", "dp"),
        P("dp", "col"),
        P("dp", "col"),
        P("col", "dp"),
        P("dp", "col"),
        P("dp", "col"),
        P("col", "dp"),
        P("col"),
    )
    out_specs = (P("col", "dp"), P("dp", "col"), P("dp", "col"), P("col", "dp"))
    return jax.shard_map(
        on_device, mesh=mesh, in_specs=in_specs, out_specs=out_specs, check_vma=False
    )
```

profile of v0, /device:TPU:0, one launch (start us, length us, event | category | flops | bytes accessed | tf_op | source)
XLA Modules:
  0.0 395.8 jit_solution(8726579454171122855)
XLA Ops:
  7.2 0.0 all-gather.5.cloned.1.call-start
  7.2 0.7 all-gather.5.cloned.1.call-update
  7.9 0.0 all-gather.9.cloned.1.call-start
  8.6 1.7 broadcast_select_fusion
  10.3 0.0 all-gather.9.cloned.1.call-update
  10.4 0.0 reduce-scatter.10.cloned.1.call-start
  10.4 0.7 broadcast_compare_fusion.1
  11.1 0.1 copy.33
  11.2 0.7 broadcast_compare_fusion.2
  11.9 0.1 copy.31
  12.0 10.4 %copy.32 = bf16[1024,3584]{0,1:T(8,128)(2,1)} copy(bf16[1024,3584]{1,0:T(8,128)(2,1)} %param.11) | data formatting | bytes 14680064 | tf_op args[2]
  22.4 10.4 %copy.34 = bf16[1024,3584]{0,1:T(8,128)(2,1)} copy(bf16[1024,3584]{1,0:T(8,128)(2,1)} %param.12) | data formatting | bytes 14680064 | tf_op args[3]
  32.8 0.0 copy-start.4
  32.8 1.0 broadcast_in_dim.78
  33.9 0.0 copy-start
  33.9 1.0 broadcast_in_dim.76
  34.9 0.0 copy-start.2
  34.9 0.8 copy-done
  35.7 1.9 copy-done.2
  37.6 1.0 copy-done.4
  38.6 10.1 %bitcast_select_fusion.2 = (bf16[1024,3584]{0,1:T(8,128)(2,1)}, bf16[1024,3584]{0,1:T(8,128)(2,1)}) fusion(bf16[1024,3584]{0,1:T(8,128)(2,1)} %copy.34, pred[448,8,8,128]{3,2,1,0:T(8,128)(4,1)S(1)} %bitcast.38, bf16[1024,3584]{0,1:T(8,128)(2,1)S(1)} %copy-done.4, pred[448,8,8,128]{3,2,1,0:T(8,128)(4,1)S(1)} %bitcast.40), kind=kLoop, calls=%fused_computation.9 | loop fusion | flops 7340032 | bytes 36700160 | tf_op jit(solution)/shard_map/jit(_where)/select_n | solution.py:13
  48.6 0.0 all-gather.5.cloned.1.call-done
  48.6 16.4 %fusion.7 = bf16[512,7168]{0,1:T(8,128)(2,1)} fusion(bf16[512,1024]{1,0:T(8,128)(2,1)} %all-gather.5.cloned.1.call-done, bf16[1024,3584]{0,1:T(8,128)(2,1)} %get-tuple-element.21, bf16[1024,3584]{0,1:T(8,128)(2,1)} %get-tuple-element.22), kind=kOutput, calls=%fused_computation.12 | convolution fusion | flops 7549222912 | bytes 23068672 | tf_op jit(solution)/shard_map/dot_general | solution.py:50
  65.1 9.9 %copy.41 = bf16[512,7168]{1,0:T(8,128)(2,1)} copy(bf16[512,7168]{0,1:T(8,128)(2,1)} %fusion.7) | data formatting | bytes 14680064
  75.0 0.0 copy-start.6
  75.0 0.0 reduce-scatter.10.cloned.1.call-update
  75.0 0.0 reduce-scatter.12.cloned.1.call-start
  75.1 0.6 copy-done.6
  75.7 0.1 copy.36
  75.8 0.0 all-gather.9.cloned.1.call-done
  75.8 1.0 broadcast_in_dim.80
  76.8 0.0 copy-start.5
  76.9 1.8 copy-done.5
  78.7 9.5 %convolution_convert_fusion = bf16[512,3584]{1,0:T(8,128)(2,1)} fusion(bf16[512,1024]{1,0:T(8,128)(2,1)} %all-gather.9.cloned.1.call-done, bf16[3584,1024]{1,0:T(8,128)(2,1)} %param.13, pred[448,8,8,128]{3,2,1,0:T(8,128)(4,1)S(1)} %bitcast.42), kind=kOutput, calls=%fused_computation.13 | convolution fusion | flops 3763601408 | bytes 15728640 | tf_op jit(solution)/shard_map/dot_general | solution.py:59
  88.2 0.0 reduce-scatter.12.cloned.1.call-update
  88.3 0.0 all-gather.7.cloned.1.call-start
  88.3 56.4 %reduce-scatter.10.cloned.1.call-done = bf16[64,7168]{1,0:T(8,128)(2,1)} async-done(((bf16[512,7168]{1,0:T(8,128)(2,1)}), bf16[64,7168]{1,0:T(8,128)(2,1)}) %reduce-scatter.10.cloned.1.call-update) | async-done | bytes 917520 | tf_op jit(solution)/shard_map/reduce_scatter | solution.py:49
  144.7 1.3 convert_element_type.35
  146.0 51.7 %reduce-scatter.12.cloned.1.call-done = bf16[64,3584]{1,0:T(8,128)(2,1)} async-done(((bf16[512,3584]{1,0:T(8,128)(2,1)}), bf16[64,3584]{1,0:T(8,128)(2,1)}) %reduce-scatter.12.cloned.1.call-update) | async-done | bytes 458768 | tf_op jit(solution)/shard_map/reduce_scatter | solution.py:58
  197.7 2.3 fusion.16
  200.0 0.0 all-gather.7.cloned.1.call-update
  200.0 0.0 reduce-scatter.8.cloned.1.call-start
  200.1 34.6 %all-gather.7.cloned.1.call-done = bf16[512,3584]{1,0:T(8,128)(2,1)} async-done(((bf16[64,3584]{1,0:T(8,128)(2,1)}), bf16[512,3584]{1,0:T(8,128)(2,1)}) %all-gather.7.cloned.1.call-update) | async-done | bytes 3670032 | tf_op jit(solution)/shard_map/all_gather | solution.py:56
  234.7 10.1 %fusion.13 = bf16[512,1024]{1,0:T(8,128)(2,1)} fusion(bf16[512,3584]{1,0:T(8,128)(2,1)} %all-gather.7.cloned.1.call-done, bf16[3584,1024]{1,0:T(8,128)(2,1)} %param.13, pred[448,8,8,128]{3,2,1,0:T(8,128)(4,1)} %bitcast.43), kind=kOutput, calls=%fused_computation.17 | convolution fusion | flops 3762290688 | bytes 15728640 | tf_op jit(solution)/shard_map/dot_general | solution.py:76
  244.8 0.0 reduce-scatter.8.cloned.1.call-update
  244.8 0.3 all-gather.11.cloned.1.call-start
  245.1 1.0 pad_maximum_fusion
  246.1 0.0 all-gather.11.cloned.1.call-update
  246.1 0.0 copy-start.7
  246.1 13.6 %bitcast_select_fusion = f32[3584,1024]{1,0:T(8,128)} fusion(pred[448,8,8,128]{3,2,1,0:T(8,128)(4,1)} %bitcast.44, bf16[512,3584]{1,0:T(8,128)(2,1)} %all-gather.7.cloned.1.call-done, bf16[512,1024]{1,0:T(8,128)(2,1)} %all-gather.9.cloned.1.call-done), kind=kOutput, calls=%fused_computation.7 | convolution fusion | flops 3761766400 | bytes 23068672 | tf_op jit(solution)/shard_map/dot_general | solution.py:82
  259.7 12.4 %reduce-scatter.8.cloned.1.call-done = bf16[128,1024]{1,0:T(8,128)(2,1)} async-done(((bf16[512,1024]{1,0:T(8,128)(2,1)}), bf16[128,1024]{1,0:T(8,128)(2,1)}) %reduce-scatter.8.cloned.1.call-update) | async-done | bytes 262160 | tf_op jit(solution)/shard_map/reduce_scatter | solution.py:75
  272.1 1.8 select_convert_fusion
  273.9 48.9 %all-gather.11.cloned.1.call-done = bf16[512,7168]{1,0:T(8,128)(2,1)} async-done(((bf16[64,7168]{1,0:T(8,128)(2,1)}), bf16[512,7168]{1,0:T(8,128)(2,1)}) %all-gather.11.cloned.1.call-update) | async-done | bytes 7340048 | tf_op jit(solution)/shard_map/all_gather | solution.py:70
  322.8 0.0 copy-done.7
  322.8 0.0 copy-start.1
  322.8 0.0 copy-start.3
  322.8 16.8 %convolution_bitcast_fusion = f32[1024,7168]{0,1:T(8,128)} fusion(bf16[512,7168]{1,0:T(8,128)(2,1)} %all-gather.11.cloned.1.call-done, bf16[512,1024]{1,0:T(8,128)(2,1)S(1)} %copy-done.7), kind=kOutput, calls=%fused_computation | convolution fusion | flops 7516192768 | bytes 37748736 | tf_op jit(solution)/shard_map/dot_general | solution.py:68
  339.6 0.0 copy-done.1
  339.6 0.0 copy-done.3
  339.7 20.8 %slice_select_fusion = (f32[1024,3584]{0,1:T(8,128)}, f32[1024,3584]{0,1:T(8,128)}) fusion(f32[1024,7168]{0,1:T(8,128)} %convolution_bitcast_fusion, pred[448,8,8,128]{3,2,1,0:T(8,128)(4,1)S(1)} %bitcast.39, pred[448,8,8,128]{3,2,1,0:T(8,128)(4,1)S(1)} %bitcast.41), kind=kLoop, calls=%fused_computation.1 | loop fusion | flops 7340032 | bytes 66060288 | tf_op jit(solution)/shard_map/jit(_where)/select_n | solution.py:13
  360.4 14.3 %copy.39 = f32[1024,3584]{1,0:T(8,128)} copy(f32[1024,3584]{0,1:T(8,128)} %get-tuple-element.17) | data formatting | bytes 29360128
  374.7 14.3 %copy.40 = f32[1024,3584]{1,0:T(8,128)} copy(f32[1024,3584]{0,1:T(8,128)} %get-tuple-element.16) | data formatting | bytes 29360128
  (2 shorter events, 0.0 us)
Async XLA Ops:
  7.2 41.5 %all-gather.5.cloned.1.call-start = ((), (), s32[]{:S(2)}) async-start(), calls=%async_computation.3 | async-start | bytes 1310720 | tf_op jit(solution)/shard_map/all_gather | solution.py:38
  7.9 67.9 %all-gather.9.cloned.1.call-start = ((), (), s32[]{:S(2)}) async-start(), calls=%async_computation.6 | async-start | bytes 1310720 | tf_op jit(solution)/shard_map/all_gather | solution.py:39
  10.4 134.3 %reduce-scatter.10.cloned.1.call-start = ((), (), s32[]{:S(2)}) async-start(), calls=%async_computation.8 | async-start | bytes 8257536 | tf_op jit(solution)/shard_map/reduce_scatter | solution.py:49
  32.8 5.7 %copy-start.4 = (bf16[1024,3584]{0,1:T(8,128)(2,1)S(1)}, bf16[1024,3584]{0,1:T(8,128)(2,1)}, u32[]{:S(2)}) copy-start(bf16[1024,3584]{0,1:T(8,128)(2,1)} %copy.32) | copy-start | bytes 22020100
  33.9 1.9 copy-start
  34.9 2.7 copy-start.2
  75.0 0.7 copy-start.6
  75.0 122.7 %reduce-scatter.12.cloned.1.call-start = ((), (), s32[]{:S(2)}) async-start(), calls=%async_computation.9 | async-start | bytes 4128768 | tf_op jit(solution)/shard_map/reduce_scatter | solution.py:58
  76.8 1.8 copy-start.5
  88.3 146.4 %all-gather.7.cloned.1.call-start = ((), (), s32[]{:S(2)}) async-start(), calls=%async_computation.4 | async-start | bytes 4128768 | tf_op jit(solution)/shard_map/all_gather | solution.py:56
  200.0 72.1 %reduce-scatter.8.cloned.1.call-start = ((), (), s32[]{:S(2)}) async-start(), calls=%async_computation.5 | async-start | bytes 1310720 | tf_op jit(solution)/shard_map/reduce_scatter | solution.py:75
  244.8 78.0 %all-gather.11.cloned.1.call-start = ((), (), s32[]{:S(2)}) async-start(), calls=%async_computation.7 | async-start | bytes 8257536 | tf_op jit(solution)/shard_map/all_gather | solution.py:70
  246.1 76.7 %copy-start.7 = (bf16[512,1024]{1,0:T(8,128)(2,1)S(1)}, bf16[512,1024]{1,0:T(8,128)(2,1)}, u32[]{:S(2)}) copy-start(bf16[512,1024]{1,0:T(8,128)(2,1)} %all-gather.5.cloned.1.call-done) | copy-start | bytes 3145732
  322.8 16.8 %copy-start.1 = (pred[8,128,28,128]{1,0,3,2:T(8,128)(4,1)S(1)}, pred[8,128,28,128]{1,0,3,2:T(8,128)(4,1)}, u32[]{:S(2)}) copy-start(pred[8,128,28,128]{1,0,3,2:T(8,128)(4,1)} %copy-done) | copy-start | bytes 11010052
  322.8 16.8 %copy-start.3 = (pred[8,128,28,128]{1,0,3,2:T(8,128)(4,1)S(1)}, pred[8,128,28,128]{1,0,3,2:T(8,128)(4,1)}, u32[]{:S(2)}) copy-start(pred[8,128,28,128]{1,0,3,2:T(8,128)(4,1)} %copy-done.2) | copy-start | bytes 11010052
Sparse Core Ops, SparseCore 0:
  9.6 30.6 all-gather.4
  42.4 27.4 all-gather.8
  75.2 69.4 reduce-scatter.9
  148.9 48.7 reduce-scatter.11
  200.1 34.4 all-gather.6
  245.0 27.1 reduce-scatter.7
  274.2 48.5 all-gather.10
where the time goes:
time: 397 us; the launch traced here: 396 us
  waiting for transfers between devices  205 us (52%)
  local copies, waits for them, and re-layouts  68.8 us (17%)
  matrix products  66.5 us (17%)
  other arithmetic  40.3 us (10%)
  between operations  14.9 us (4%)
    unnamed x21, local copies, waits for them, and re-layouts  65.4 us
    reduce_scatter x1, waiting for transfers between devices, on_device(): lax.psum_scatter(jnp.dot(block, w_both, preferred_element_type=jnp.float3...  56.4 us
    reduce_scatter x1, waiting for transfers between devices, on_device(): lax.psum_scatter(lax.dot_general(block, w_down, contract_cols, preferred_...  51.7 us
    all_gather x1, waiting for transfers between devices, on_device(): lax.all_gather(d_mine, 'dp', axis=0, tiled=True)  48.9 us
    all_gather x1, waiting for transfers between devices, on_device(): hidden_all = lax.all_gather(hidden_mine, 'dp', axis=0, tiled=True)  34.6 us
    select_n x2, other arithmetic, widen(): return jnp.where(keep, shaped, jnp.zeros_like(shaped)).reshape(weight.shape)  30.8 us
    dot_general x1, matrix products, on_device(): lax.dot_general(block, lax.all_gather(d_mine, 'dp', axis=0, tiled=True),...  16.8 us
    dot_general x1, matrix products, on_device(): jnp.dot(block, w_both, preferred_element_type=jnp.float32)  16.4 us
  transfers between devices with their start and end apart: 7, of which 5 were waited for; matrix products, arithmetic and copies ran while one was open for 23% of the time, Pallas kernels for 0%

commit v1 on v0

v1 whole, which is shorter than its diff:
```python
import functools

import jax
import jax.numpy as jnp
from jax import lax
from jax.experimental import pallas as pl
from jax.experimental.pallas import tpu as pltpu
from jax.sharding import PartitionSpec as P

MESH = pl.DeviceIdType.MESH
BLOCK = 128
F32 = jnp.float32
BF16 = jnp.bfloat16


class Plan:
    def __init__(self, n_col, n_dp, tok_dev, feats, units):
        self.n_col, self.n_dp, self.tok_dev, self.feats, self.units = n_col, n_dp, tok_dev, feats, units
        self.levels = n_dp.bit_length() - 1
        self.rows = n_col * tok_dev * 3 // 4
        self.piece = self.rows // n_dp
        half = units // 2
        self.wide = 256 if half % 256 == 0 else BLOCK
        self.per_path = half // self.wide
        self.chunks = 2 * self.per_path
        k = self.levels
        self.bits = [list(range(k)), [0] + list(range(k - 1, 0, -1))]
        self.orders = []
        for bits in self.bits:
            order = []
            for place in range(n_dp):
                owner = 0
                for level, bit in enumerate(bits):
                    if place >> (k - 1 - level) & 1:
                        owner |= 1 << bit
                order.append(owner)
            self.orders.append(order)


def bit_of(index, bit):
    return (index // (1 << bit)) % 2


def partner_of(index, bit):
    return index + (1 - 2 * bit_of(index, bit)) * (1 << bit)


def exchange_kernel(
    plan,
    cnt_ref, tok_ref, cot_ref, gate_mask, up_mask, down_mask, wg_hbm, wu_hbm, wd_hbm,
    out_ref, tokc, gc, hid_out, d_out,
    cnt_all, tok_all, cot_all, place, wg, wu, wd, w_sem,
    keep, s0, r0, s1, r1, bkeep, bs0, br0, bs1, br1,
    hid, dd, acc, zs, zr,
    ring_sem, gu_sem, bk_sem, hid_sem, d_sem, z_sem, out_sem,
):
    n_col, k, td, wide = plan.n_col, plan.levels, plan.tok_dev, plan.wide
    rows, piece, per, chunks = plan.rows, plan.piece, plan.per_path, plan.chunks
    col, dp = lax.axis_index("col"), lax.axis_index("dp")

    def remote(src, dst, sems, at, **to):
        return pltpu.make_async_remote_copy(
            src_ref=src,
            dst_ref=dst,
            send_sem=sems.at[(0, *at)],
            recv_sem=sems.at[(1, *at)],
            device_id=(to.get("col", col), to.get("dp", dp)),
            device_id_type=MESH,
        )

    def weight_copies(u):
        cols = pl.ds(pl.multiple_of(u * wide, wide), wide)
        return (
            pltpu.make_async_copy(wg_hbm.at[:, cols], wg.at[u], w_sem.at[0, u]),
            pltpu.make_async_copy(wu_hbm.at[:, cols], wu.at[u], w_sem.at[1, u]),
            pltpu.make_async_copy(wd_hbm.at[cols, :], wd.at[u], w_sem.at[2, u]),
        )

    @pl.loop(0, chunks)
    def _(u):
        for copy in weight_copies(u):
            copy.start()

    barrier = pltpu.get_barrier_semaphore()
    for bit in range(k):
        pl.semaphore_signal(
            barrier, inc=1, device_id=(col, partner_of(dp, bit)), device_id_type=MESH
        )
    for step in range(1, n_col):
        pl.semaphore_signal(
            barrier, inc=1, device_id=((col + step) % n_col, dp), device_id_type=MESH
        )
    pl.semaphore_wait(barrier, k + n_col - 1)

    cnt_all[col] = cnt_ref[...]
    tok_all[col] = tok_ref[...]
    live = lax.broadcasted_iota(jnp.int32, (td, plan.feats), 0) < cnt_ref[0:1, 0:1]
    cot_all[col] = jnp.where(live, cot_ref[...].astype(F32), 0.0).astype(BF16)

    def hop(bufs, way, step, name):
        first, last = bufs
        block = col - step if way == 0 else col + step
        to = col + 1 if way == 0 else col - 1
        return [
            remote(buf.at[block], buf.at[block], ring_sem, (first + i, way, step), col=to)
            for i, buf in enumerate(last)
        ]

    def sends(way, step):
        return (
            (col - step >= 0) & (col + 1 < n_col) if way == 0 else (col + step < n_col) & (col >= 1)
        )

    def receives(way, step):
        return col - 1 - step >= 0 if way == 0 else col + 1 + step < n_col

    def hop_start(bufs, step):
        for way in range(2):

            @pl.when(sends(way, step))
            def _():
                for copy in hop(bufs, way, step, "s"):
                    copy.start()

    def hop_wait_recv(bufs, step):
        for way in range(2):

            @pl.when(receives(way, step))
            def _():
                first, last = bufs
                block = col - 1 - step if way == 0 else col + 1 + step
                for i, buf in enumerate(last):
                    remote(
                        buf.at[block], buf.at[block], ring_sem, (first + i, way, step), col=block
                    ).wait_recv()

    def hop_wait_send(bufs, step):
        for way in range(2):

            @pl.when(sends(way, step))
            def _():
                for copy in hop(bufs, way, step, "w"):
                    copy.wait_send()

    tok_bufs = (0, [tok_all, cnt_all])
    cot_bufs = (2, [cot_all])
    hop_start(tok_bufs, 0)

    side, parts = plan.feats // BLOCK, wide // BLOCK

    @pl.loop(0, chunks)
    def _(u):
        for copy in weight_copies(u):
            copy.wait()
        for r in range(side):
            for c in range(parts):
                at = (u, pl.ds(r * BLOCK, BLOCK), pl.ds(c * BLOCK, BLOCK))
                turned = (u, pl.ds(c * BLOCK, BLOCK), pl.ds(r * BLOCK, BLOCK))
                wg[at] = wg[at] * (gate_mask[r, u * parts + c] > 0).astype(F32).astype(BF16)
                wu[at] = wu[at] * (up_mask[r, u * parts + c] > 0).astype(F32).astype(BF16)
                wd[turned] = wd[turned] * (down_mask[u * parts + c, r] > 0).astype(F32).astype(BF16)

    for step in range(1, n_col - 1):
        hop_wait_recv(tok_bufs, step - 1)
        hop_start(tok_bufs, step)
    hop_wait_recv(tok_bufs, n_col - 2)
    hop_start(cot_bufs, 0)

    lane = lax.broadcasted_iota(jnp.int32, (piece, td), 1)
    row = lax.broadcasted_iota(jnp.int32, (piece, td), 0)
    before = jnp.zeros((1, td), jnp.int32)
    for shard in range(n_col):
        count = cnt_all[shard][0:1, :]
        for path in range(2):
            for i, owner in enumerate(plan.orders[path]):
                target = 0
                for bit in range(k):
                    mine = bit_of(dp, bit)
                    target = target + (1 - mine if owner >> bit & 1 else mine) * (1 << bit)
                hit = (row + target * piece - before == lane) & (lane < count)
                place[path, i * piece : (i + 1) * piece, shard * td : (shard + 1) * td] = jnp.where(
                    hit, 1.0, 0.0
                ).astype(BF16)
        before = before + count

    def compact(buf, to):
        for path in range(2):
            total = None
            for shard in range(n_col):
                part = jnp.dot(
                    place[path, :, shard * td : (shard + 1) * td],
                    buf[shard],
                    preferred_element_type=F32,
                )
                total = part if total is None else total + part
            to[path] = total.astype(BF16)

    compact(tok_all, tokc)

    class Scatter:
        def __init__(self, keep, s0, r0, s1, r1, sem):
            self.keep, self.bufs, self.sem = keep, ((s0, r0), (s1, r1)), sem

        def copy(self, path, level, u):
            size = rows >> (level + 1)
            src, dst = self.bufs[min(level, 1)]
            start = 0 if level == 0 else (rows >> 1) - (rows >> level)
            at = (u, pl.ds(start, size))
            return remote(
                src.at[at], dst.at[at], self.sem, (level, u),
                dp=partner_of(dp, plan.bits[path][level]),
            )

        def put(self, path, u, value):
            half = rows >> 1
            src, _ = self.bufs[0]
            src[u] = value[half:].astype(BF16)
            self.keep[u] = value[:half]
            self.copy(path, 0, u).start()

        def got(self, path, level, u):
            copy = self.copy(path, level, u)
            copy.wait_recv()
            size = rows >> (level + 1)
            _, dst = self.bufs[min(level, 1)]
            start = 0 if level == 0 else (rows >> 1) - (rows >> level)
            return self.keep[u, 0:size] + dst[u, pl.ds(start, size)].astype(F32)

        def step(self, path, level, u):
            value = self.got(path, level - 1, u)
            size = rows >> (level + 1)
            start = (rows >> 1) - (rows >> level)
            src, _ = self.bufs[1]
            src[u, pl.ds(start, size)] = value[size:].astype(BF16)
            self.keep[u, 0:size] = value[:size]
            self.copy(path, level, u).start()

    gu = Scatter(keep, s0, r0, s1, r1, gu_sem)
    bk = Scatter(bkeep, bs0, br0, bs1, br1, bk_sem)

    def gather_copy(buf, sem, path, level, u):
        size = rows >> (level + 1)
        return remote(
            buf.at[u, pl.ds(0, size)], buf.at[u, pl.ds(size, size)], sem, (level, u),
            dp=partner_of(dp, plan.bits[path][level]),
        )

    def both(body):
        for path in range(2):
            body(path)

    @pl.loop(0, per)
    def _(j):
        for path in range(2):
            u = path * per + j
            left = tokc[path]
            value = jnp.concatenate(
                [
                    jnp.dot(left, wg[u], preferred_element_type=F32),
                    jnp.dot(left, wu[u], preferred_element_type=F32),
                ],
                axis=1,
            )
            gu.put(path, u, value)

        @pl.when(j >= 1)
        def _():
            for path in range(2):
                gu.step(path, 1, path * per + j - 1)

    for path in range(2):
        gu.step(path, 1, path * per + per - 1)

    for step in range(1, n_col - 1):
        hop_wait_recv(cot_bufs, step - 1)
        hop_start(cot_bufs, step)
    if k > 2:

        @pl.loop(0, per)
        def _(j):
            for path in range(2):
                gu.step(path, 2, path * per + j)

    hop_wait_recv(cot_bufs, n_col - 2)
    compact(cot_all, gc)

    @pl.loop(0, per)
    def _(j):
        for path in range(2):
            u = path * per + j
            value = lax.dot_general(
                gc[path], wd[u], (((1,), (1,)), ((), ())), preferred_element_type=F32
            )
            bk.put(path, u, value)

        @pl.when(j >= 1)
        def _():
            for path in range(2):
                bk.step(path, 1, path * per + j - 1)

    for path in range(2):
        bk.step(path, 1, path * per + per - 1)

    for level in range(3, k):

        @pl.loop(0, per)
        def _(j):
            for path in range(2):
                gu.step(path, level, path * per + j)

    @pl.loop(0, per)
    def _(j):
        for path in range(2):
            u = path * per + j
            value = gu.got(path, k - 1, u)
            keep[u, 0:piece] = value
            gate, upward = value[:, :wide], value[:, wide:]
            sigma = 1.0 / (1.0 + jnp.exp(-gate))
            hid[u, 0:piece] = (gate * sigma * upward).astype(BF16)
            gather_copy(hid, hid_sem, path, k - 1, u).start()

    for level in range(2, k):

        @pl.loop(0, per)
        def _(j):
            for path in range(2):
                bk.step(path, level, path * per + j)

    def gather_step(buf, sem, level):
        @pl.loop(0, per)
        def _(j):
            for path in range(2):
                u = path * per + j
                gather_copy(buf, sem, path, level + 1, u).wait_recv()
                gather_copy(buf, sem, path, level, u).start()

    gather_step(hid, hid_sem, k - 2)

    @pl.loop(0, per)
    def _(j):
        for path in range(2):
            u = path * per + j
            back = bk.got(path, k - 1, u)
            gate, upward = keep[u, 0:piece, 0:wide], keep[u, 0:piece, wide : 2 * wide]
            sigma = 1.0 / (1.0 + jnp.exp(-gate))
            dd[u, 0:piece, 0:wide] = (
                back * upward * sigma * (1.0 + gate * (1.0 - sigma))
            ).astype(BF16)
            dd[u, 0:piece, wide : 2 * wide] = (back * (gate * sigma)).astype(BF16)
            gather_copy(dd, d_sem, path, k - 1, u).start()

    for level in range(k - 3, -1, -1):
        gather_step(hid, hid_sem, level)
    gather_step(dd, d_sem, k - 2)

    acc[...] = jnp.zeros_like(acc)

    @pl.loop(0, per)
    def _(j):
        for path in range(2):
            u = path * per + j
            gather_copy(hid, hid_sem, path, 0, u).wait_recv()
            pltpu.make_async_copy(hid.at[u], hid_out.at[u], out_sem.at[0, u]).start()
            acc[path] += jnp.dot(hid[u], wd[u], preferred_element_type=F32)

    for i, owner in enumerate(plan.orders[0]):
        other = plan.orders[1].index(owner)
        at = pl.ds(i * piece, piece)
        acc[0, at] = acc[0, at] + acc[1, pl.ds(other * piece, piece)]
    mixed = acc[0].astype(BF16)
    for shard in range(n_col):
        zs[shard] = lax.dot_general(
            place[0, :, shard * td : (shard + 1) * td],
            mixed,
            (((0,), (0,)), ((), ())),
            preferred_element_type=F32,
        ).astype(BF16)

    def z_copy(step):
        to = (col + step) % n_col
        return remote(zs.at[to], zr.at[step - 1], z_sem, (step - 1,), col=to)

    for step in range(1, n_col):
        z_copy(step).start()

    for level in range(k - 3, -1, -1):
        gather_step(dd, d_sem, level)

    @pl.loop(0, per)
    def _(j):
        for path in range(2):
            u = path * per + j
            gather_copy(dd, d_sem, path, 0, u).wait_recv()
            pltpu.make_async_copy(dd.at[u], d_out.at[u], out_sem.at[1, u]).start()

    total = zs[col].astype(F32)
    for step in range(1, n_col):
        z_copy(step).wait_recv()
        total = total + zr[step - 1].astype(F32)
    out_ref[...] = total.astype(BF16)

    for step in range(1, n_col):
        z_copy(step).wait_send()
    for step in range(n_col - 1):
        hop_wait_send(tok_bufs, step)
        hop_wait_send(cot_bufs, step)

    @pl.loop(0, per)
    def _(j):
        for path in range(2):
            u = path * per + j
            for level in range(k):
                gu.copy(path, level, u).wait_send()
                bk.copy(path, level, u).wait_send()
                gather_copy(hid, hid_sem, path, level, u).wait_send()
                gather_copy(dd, d_sem, path, level, u).wait_send()
            pltpu.make_async_copy(hid.at[u], hid_out.at[u], out_sem.at[0, u]).wait()
            pltpu.make_async_copy(dd.at[u], d_out.at[u], out_sem.at[1, u]).wait()


def exchange(plan, cnt, tokens, cotangent, gate_mask, up_mask, down_mask, wg, wu, wd):
    n_col, k, td, wide = plan.n_col, plan.levels, plan.tok_dev, plan.wide
    rows, chunks, feats = plan.rows, plan.chunks, plan.feats
    vmem, smem = pl.BlockSpec(memory_space=pltpu.VMEM), pl.BlockSpec(memory_space=pltpu.SMEM)
    whole = pl.BlockSpec(memory_space=pl.ANY)
    half = rows // 2
    rest = half - (rows >> k)

    def scatter_bufs(width):
        return [
            pltpu.VMEM((chunks, half, width), F32),
            pltpu.VMEM((chunks, half, width), BF16),
            pltpu.VMEM((chunks, half, width), BF16),
            pltpu.VMEM((chunks, rest, width), BF16),
            pltpu.VMEM((chunks, rest, width), BF16),
        ]

    return pl.pallas_call(
        functools.partial(exchange_kernel, plan),
        out_shape=(
            jax.ShapeDtypeStruct((td, feats), BF16),
            jax.ShapeDtypeStruct((2, rows, feats), BF16),
            jax.ShapeDtypeStruct((2, rows, feats), BF16),
            jax.ShapeDtypeStruct((chunks, rows, wide), BF16),
            jax.ShapeDtypeStruct((chunks, rows, 2 * wide), BF16),
        ),
        in_specs=[vmem, vmem, vmem, smem, smem, smem, whole, whole, whole],
        out_specs=(vmem, vmem, vmem, whole, whole),
        scratch_shapes=[
            pltpu.VMEM((n_col, 8, 128), jnp.int32),
            pltpu.VMEM((n_col, td, feats), BF16),
            pltpu.VMEM((n_col, td, feats), BF16),
            pltpu.VMEM((2, rows, n_col * td), BF16),
            pltpu.VMEM((chunks, feats, wide), BF16),
            pltpu.VMEM((chunks, feats, wide), BF16),
            pltpu.VMEM((chunks, wide, feats), BF16),
            pltpu.SemaphoreType.DMA((3, chunks)),
            *scatter_bufs(2 * wide),
            *scatter_bufs(wide),
            pltpu.VMEM((chunks, rows, wide), BF16),
            pltpu.VMEM((chunks, rows, 2 * wide), BF16),
            pltpu.VMEM((2, rows, feats), F32),
            pltpu.VMEM((n_col, td, feats), BF16),
            pltpu.VMEM((n_col - 1, td, feats), BF16),
            pltpu.SemaphoreType.DMA((2, 3, 2, n_col - 1)),
            pltpu.SemaphoreType.DMA((2, k, chunks)),
            pltpu.SemaphoreType.DMA((2, k, chunks)),
            pltpu.SemaphoreType.DMA((2, k, chunks)),
            pltpu.SemaphoreType.DMA((2, k, chunks)),
            pltpu.SemaphoreType.DMA((2, n_col - 1)),
            pltpu.SemaphoreType.DMA((2, chunks)),
        ],
        compiler_params=pltpu.CompilerParams(
            collective_id=0, has_side_effects=True, vmem_limit_bytes=63 * 2**20
        ),
    )(cnt, tokens, cotangent, gate_mask, up_mask, down_mask, wg, wu, wd)


def grads_kernel(
    plan, gate_mask, up_mask, down_mask, tokc, gc, hid, dd, gate_grad, up_grad, down_grad, turned
):
    u = pl.program_id(0)
    wide = plan.wide
    side, parts = plan.feats // BLOCK, wide // BLOCK

    @pl.when((u == 0) | (u == plan.per_path))
    def _():
        turned[...] = tokc[0].T

    def keep(mask, value):
        return jnp.where(mask > 0, value, 0.0)

    for ref, mask, lo in ((gate_grad, gate_mask, 0), (up_grad, up_mask, wide)):
        value = jnp.dot(turned[...], dd[0, :, lo : lo + wide], preferred_element_type=F32)
        for r in range(side):
            for c in range(parts):
                rs, cs = slice(r * BLOCK, (r + 1) * BLOCK), slice(c * BLOCK, (c + 1) * BLOCK)
                ref[rs, cs] = keep(mask[r, u * parts + c], value[rs, cs])
    value = jnp.dot(hid[0].T, gc[0], preferred_element_type=F32)
    for r in range(side):
        for c in range(parts):
            rs, cs = slice(r * BLOCK, (r + 1) * BLOCK), slice(c * BLOCK, (c + 1) * BLOCK)
            down_grad[cs, rs] = keep(down_mask[u * parts + c, r], value[cs, rs])


def grads(plan, gate_mask, up_mask, down_mask, tokc, gc, hid, dd):
    rows, feats, wide, per = plan.rows, plan.feats, plan.wide, plan.per_path
    smem = pl.BlockSpec(memory_space=pltpu.SMEM)
    return pl.pallas_call(
        functools.partial(grads_kernel, plan),
        grid=(plan.chunks,),
        out_shape=(
            jax.ShapeDtypeStruct((feats, plan.units), F32),
            jax.ShapeDtypeStruct((feats, plan.units), F32),
            jax.ShapeDtypeStruct((plan.units, feats), F32),
        ),
        in_specs=[
            smem,
            smem,
            smem,
            pl.BlockSpec((1, rows, feats), lambda u: (u // per, 0, 0)),
            pl.BlockSpec((1, rows, feats), lambda u: (u // per, 0, 0)),
            pl.BlockSpec((1, rows, wide), lambda u: (u, 0, 0)),
            pl.BlockSpec((1, rows, 2 * wide), lambda u: (u, 0, 0)),
        ],
        out_specs=(
            pl.BlockSpec((feats, wide), lambda u: (0, u)),
            pl.BlockSpec((feats, wide), lambda u: (0, u)),
            pl.BlockSpec((wide, feats), lambda u: (u, 0)),
        ),
        scratch_shapes=[pltpu.VMEM((feats, rows), BF16)],
        compiler_params=pltpu.CompilerParams(vmem_limit_bytes=48 * 2**20),
    )(gate_mask, up_mask, down_mask, tokc, gc, hid, dd)


def on_device(
    n_col, n_dp,
    tokens, cotangent, gate_weight, up_weight, down_weight, gate_mask, up_mask, down_mask, counts
):
    plan = Plan(n_col, n_dp, tokens.shape[0], tokens.shape[1], gate_weight.shape[1])
    cnt = jnp.broadcast_to(counts.reshape(1, 1), (8, 128))
    output, tokc, gc, hid, dd = exchange(
        plan, cnt, tokens, cotangent, gate_mask, up_mask, down_mask,
        gate_weight, up_weight, down_weight,
    )
    gate_grad, up_grad, down_grad = grads(plan, gate_mask, up_mask, down_mask, tokc, gc, hid, dd)
    return (output, gate_grad, up_grad, down_grad)


def solution(mesh):
    in_specs = (
        P("col", "dp"),
        P("col", "dp"),
        P("dp", "col"),
        P("dp", "col"),
        P("col", "dp"),
        P("dp", "col"),
        P("dp", "col"),
        P("col", "dp"),
        P("col"),
    )
    out_specs = (P("col", "dp"), P("dp", "col"), P("dp", "col"), P("col", "dp"))
    return jax.shard_map(
        functools.partial(on_device, mesh.shape["col"], mesh.shape["dp"]),
        mesh=mesh,
        in_specs=in_specs,
        out_specs=out_specs,
        check_vma=False,
    )
```

time: 397 us -> 145 us (0.37)
  waiting for transfers between devices: 205 us -> 0 us
  Pallas kernels: 0 us -> 136 us
  matrix products: 66.5 us -> 0 us
  local copies, waits for them, and re-layouts: 68.8 us -> 7.27 us
  other arithmetic: 40.3 us -> 0 us
  between operations: 14.9 us -> 1.32 us
    pallas_call x0 -> x2, Pallas kernels: none -> 136 us  [the longest x1 116 us: exchange(): pl.pallas_call(functools.partial(exchange_kernel, plan), out_shape=(jax.S...]
    reduce_scatter x3 -> x0, waiting for transfers between devices: 121 us -> none  [the longest x1 56.4 us: on_device(): lax.psum_scatter(jnp.dot(block, w_both, preferred_element_type=jnp.float3...]
    all_gather x4 -> x0, waiting for transfers between devices: 83.5 us -> none  [the longest x1 48.9 us: on_device(): lax.all_gather(d_mine, 'dp', axis=0, tiled=True)]
    dot_general x5 -> x0, matrix products: 66.5 us -> none  [the longest x1 16.8 us: on_device(): lax.dot_general(block, lax.all_gather(d_mine, 'dp', axis=0, tiled=True),...]
    unnamed x21 -> x16, local copies, waits for them, and re-layouts: 65.4 us -> 6.67 us
    select_n x3 -> x0, other arithmetic: 32.6 us -> none  [the longest x2 30.8 us: widen(): return jnp.where(keep, shaped, jnp.zeros_like(shaped)).reshape(weight.shape)]
    convert_element_type x3 -> x0, other arithmetic: 5.35 us -> none  [the longest x1 2.28 us: derive(): (back * upward * sigma * (1.0 + gate * (1.0 - sigma))).astype(jnp.bfloat16)]
  transfers between devices with their start and end apart: 7 -> 0, of which waited for: 5 -> 0; matrix products, arithmetic and copies ran while one was open for 23% -> 0% of each run, Pallas kernels for 0% -> 0%
where the time goes in v1:
time: 145 us
  Pallas kernels  136 us (94%)
  local copies, waits for them, and re-layouts  7.27 us (5%)
    pallas_call x1, Pallas kernels, exchange(): pl.pallas_call(functools.partial(exchange_kernel, plan), out_shape=(jax.S...  116 us
    pallas_call x1, Pallas kernels, grads(): pl.pallas_call(functools.partial(grads_kernel, plan), grid=(plan.chunks,)...  20 us
    unnamed x16, local copies, waits for them, and re-layouts  6.67 us

profile of v1, /device:TPU:0, one launch (start us, length us, event | category | flops | bytes accessed | tf_op | source)
XLA Modules:
  0.0 144.7 jit_solution(17251256365617042225)
XLA Ops:
  1.3 0.6 broadcast_in_dim.8.cnt_ref
  1.9 1.4 copy.13.down_mask
  3.2 0.0 copy-start.3
  3.2 0.0 copy-start.4
  3.2 0.0 copy-start.5
  3.2 116.2 %shard_map.120 = (bf16[128,1024]{1,0:T(8,128)(2,1)}, bf16[2,384,1024]{2,1,0:T(8,128)(2,1)}, bf16[2,384,1024]{2,1,0:T(8,128)(2,1)}, bf16[14,384,256]{2,1,0:T(8,128)(2,1)}, bf16[14,384,512]{2,1,0:T(8,128)(2,1)}) custom-call(s32[8,128]{1,0:T(8,128)} %broadcast_in_dim.8.cnt_ref, bf16[128,1024]{1,0:T(8,128)(2,1)} %tok_ref.1, bf16[128,1024]{1,0:T(8,128)(2,1)} %cot_ref.1, ...), custom_call_target="tpu_custom_call" | custom-call | tf_op jit(solution)/shard_map/pallas_call | solution.py:438
  119.4 0.0 copy-done.3
  119.4 0.0 copy-done.4
  119.5 0.0 copy-done.5
  119.5 0.0 copy-start
  119.5 1.8 %copy-done = bf16[14,384,256]{2,1,0:T(8,128)(2,1)S(1)} copy-done((bf16[14,384,256]{2,1,0:T(8,128)(2,1)S(1)}, bf16[14,384,256]{2,1,0:T(8,128)(2,1)}, u32[]{:S(2)}) %copy-start) | copy-done | bytes 2752536
  121.2 0.0 copy-start.1
  121.2 1.4 copy-done.1
  122.7 0.0 copy-start.2
  122.7 1.4 copy-done.2
  124.1 0.0 copy-start.6
  124.1 20.0 %shard_map.121 = (f32[1024,3584]{1,0:T(8,128)}, f32[1024,3584]{1,0:T(8,128)}, f32[3584,1024]{1,0:T(8,128)}) custom-call(s32[8,28]{1,0:T(8,128)S(1)} %copy-done.4, s32[8,28]{1,0:T(8,128)S(1)} %copy-done.5, s32[28,8]{1,0:T(8,128)S(1)} %copy-done.3, bf16[2,384,1024]{2,1,0:T(8,128)(2,1)S(1)} %copy-done.1, bf16[2,384,1024]{2,1,0:T(8,128)(2,1)S(1)} %copy-done.2, ...), custom_call_target="tpu_custom_call" | custom-call | tf_op jit(solution)/shard_map/pallas_call | solution.py:509
  144.0 0.0 copy-done.6
  144.0 0.7 copy.17
Async XLA Ops:
  3.2 116.2 %copy-start.3 = (s32[28,8]{1,0:T(8,128)S(1)}, s32[28,8]{1,0:T(8,128)}, u32[]{:S(2)}) copy-start(s32[28,8]{1,0:T(8,128)} %copy.13.down_mask) | copy-start | bytes 2692
  3.2 116.2 %copy-start.4 = (s32[8,28]{1,0:T(8,128)S(1)}, s32[8,28]{1,0:T(8,128)}, u32[]{:S(2)}) copy-start(s32[8,28]{1,0:T(8,128)} %gate_mask.3) | copy-start | bytes 2692
  3.2 116.2 %copy-start.5 = (s32[8,28]{1,0:T(8,128)S(1)}, s32[8,28]{1,0:T(8,128)}, u32[]{:S(2)}) copy-start(s32[8,28]{1,0:T(8,128)} %up_mask.3) | copy-start | bytes 2692
  119.5 1.8 %copy-start = (bf16[14,384,256]{2,1,0:T(8,128)(2,1)S(1)}, bf16[14,384,256]{2,1,0:T(8,128)(2,1)}, u32[]{:S(2)}) copy-start(bf16[14,384,256]{2,1,0:T(8,128)(2,1)} %get-tuple-element.15.hid) | copy-start | bytes 8257540
  121.2 1.4 copy-start.1
  122.7 1.4 copy-start.2
  124.1 20.0 %copy-start.6 = (bf16[128,1024]{1,0:T(8,128)(2,1)S(1)}, bf16[128,1024]{1,0:T(8,128)(2,1)}, u32[]{:S(2)}) copy-start(bf16[128,1024]{1,0:T(8,128)(2,1)} %get-tuple-element.24) | copy-start | bytes 786436

commit v2 on v1

--- a/solution.py
+++ b/solution.py
@@ -78,8 +78,12 @@
 
     @pl.loop(0, chunks)
     def _(u):
-        for copy in weight_copies(u):
+        for copy in weight_copies(u)[:2]:
             copy.start()
+
+    @pl.loop(0, chunks)
+    def _(u):
+        weight_copies(u)[2].start()
 
     barrier = pltpu.get_barrier_semaphore()
     for bit in range(k):
@@ -148,21 +152,32 @@
 
     side, parts = plan.feats // BLOCK, wide // BLOCK
 
-    @pl.loop(0, chunks)
-    def _(u):
-        for copy in weight_copies(u):
-            copy.wait()
-        for r in range(side):
-            for c in range(parts):
-                at = (u, pl.ds(r * BLOCK, BLOCK), pl.ds(c * BLOCK, BLOCK))
-                turned = (u, pl.ds(c * BLOCK, BLOCK), pl.ds(r * BLOCK, BLOCK))
-                wg[at] = wg[at] * (gate_mask[r, u * parts + c] > 0).astype(F32).astype(BF16)
-                wu[at] = wu[at] * (up_mask[r, u * parts + c] > 0).astype(F32).astype(BF16)
-                wd[turned] = wd[turned] * (down_mask[u * parts + c, r] > 0).astype(F32).astype(BF16)
-
+    def prune_in(lo, hi):
+        @pl.loop(lo, hi)
+        def _(u):
+            for copy in weight_copies(u)[:2]:
+                copy.wait()
+            for r in range(side):
+                for c in range(parts):
+                    at = (u, pl.ds(r * BLOCK, BLOCK), pl.ds(c * BLOCK, BLOCK))
+                    wg[at] = wg[at] * (gate_mask[r, u * parts + c] > 0).astype(F32).astype(BF16)
+                    wu[at] = wu[at] * (up_mask[r, u * parts + c] > 0).astype(F32).astype(BF16)
+
+    def prune_down():
+        @pl.loop(0, chunks)
+        def _(u):
+            weight_copies(u)[2].wait()
+            for r in range(side):
+                for c in range(parts):
+                    at = (u, pl.ds(c * BLOCK, BLOCK), pl.ds(r * BLOCK, BLOCK))
+                    wd[at] = wd[at] * (down_mask[r, u * parts + c] > 0).astype(F32).astype(BF16)
+
+    prune_in(0, per)
     for step in range(1, n_col - 1):
         hop_wait_recv(tok_bufs, step - 1)
         hop_start(tok_bufs, step)
+        if step == 1:
+            prune_in(per, chunks)
     hop_wait_recv(tok_bufs, n_col - 2)
     hop_start(cot_bufs, 0)
 
@@ -271,6 +286,8 @@
     for path in range(2):
         gu.step(path, 1, path * per + per - 1)
 
+    prune_down()
+
     for step in range(1, n_col - 1):
         hop_wait_recv(cot_bufs, step - 1)
         hop_start(cot_bufs, step)
@@ -318,13 +335,6 @@
             sigma = 1.0 / (1.0 + jnp.exp(-gate))
             hid[u, 0:piece] = (gate * sigma * upward).astype(BF16)
             gather_copy(hid, hid_sem, path, k - 1, u).start()
-
-    for level in range(2, k):
-
-        @pl.loop(0, per)
-        def _(j):
-            for path in range(2):
-                bk.step(path, level, path * per + j)
 
     def gather_step(buf, sem, level):
         @pl.loop(0, per)
@@ -335,6 +345,16 @@
                 gather_copy(buf, sem, path, level, u).start()
 
     gather_step(hid, hid_sem, k - 2)
+
+    for level in range(2, k):
+
+        @pl.loop(0, per)
+        def _(j):
+            for path in range(2):
+                bk.step(path, level, path * per + j)
+
+    for level in range(k - 3, -1, -1):
+        gather_step(hid, hid_sem, level)
 
     @pl.loop(0, per)
     def _(j):
@@ -348,10 +368,6 @@
             ).astype(BF16)
             dd[u, 0:piece, wide : 2 * wide] = (back * (gate * sigma)).astype(BF16)
             gather_copy(dd, d_sem, path, k - 1, u).start()
-
-    for level in range(k - 3, -1, -1):
-        gather_step(hid, hid_sem, level)
-    gather_step(dd, d_sem, k - 2)
 
     acc[...] = jnp.zeros_like(acc)
 
@@ -383,7 +399,7 @@
     for step in range(1, n_col):
         z_copy(step).start()
 
-    for level in range(k - 3, -1, -1):
+    for level in range(k - 2, -1, -1):
         gather_step(dd, d_sem, level)
 
     @pl.loop(0, per)
@@ -500,7 +516,7 @@
     for r in range(side):
         for c in range(parts):
             rs, cs = slice(r * BLOCK, (r + 1) * BLOCK), slice(c * BLOCK, (c + 1) * BLOCK)
-            down_grad[cs, rs] = keep(down_mask[u * parts + c, r], value[cs, rs])
+            down_grad[cs, rs] = keep(down_mask[r, u * parts + c], value[cs, rs])
 
 
 def grads(plan, gate_mask, up_mask, down_mask, tokc, gc, hid, dd):
@@ -529,7 +545,7 @@
             pl.BlockSpec((wide, feats), lambda u: (u, 0)),
         ),
         scratch_shapes=[pltpu.VMEM((feats, rows), BF16)],
-        compiler_params=pltpu.CompilerParams(vmem_limit_bytes=48 * 2**20),
+        compiler_params=pltpu.CompilerParams(vmem_limit_bytes=63 * 2**20),
     )(gate_mask, up_mask, down_mask, tokc, gc, hid, dd)
 
 
@@ -539,6 +555,7 @@
 ):
     plan = Plan(n_col, n_dp, tokens.shape[0], tokens.shape[1], gate_weight.shape[1])
     cnt = jnp.broadcast_to(counts.reshape(1, 1), (8, 128))
+    down_mask = down_mask.T
     output, tokc, gc, hid, dd = exchange(
         plan, cnt, tokens, cotangent, gate_mask, up_mask, down_mask,
         gate_weight, up_weight, down_weight,

time: 145 us -> 137 us (0.945)
  local copies, waits for them, and re-layouts: 7.27 us -> 1.3 us
  Pallas kernels: 136 us -> 134 us
    unnamed x16 -> x3, local copies, waits for them, and re-layouts: 6.67 us -> 0.71 us
    pallas_call x1, Pallas kernels: 116 us -> 111 us  [exchange(): pl.pallas_call(functools.partial(exchange_kernel, plan), out_shape=(jax.S...]
    pallas_call x1, Pallas kernels: 20 us -> 23.4 us  [grads(): pl.pallas_call(functools.partial(grads_kernel, plan), grid=(plan.chunks,)...]
where the time goes in v2:
time: 137 us
  Pallas kernels  134 us (98%)
    pallas_call x1, Pallas kernels, exchange(): pl.pallas_call(functools.partial(exchange_kernel, plan), out_shape=(jax.S...  111 us
    pallas_call x1, Pallas kernels, grads(): pl.pallas_call(functools.partial(grads_kernel, plan), grid=(plan.chunks,)...  23.4 us

profile of v2, /device:TPU:0, one launch (start us, length us, event | category | flops | bytes accessed | tf_op | source)
XLA Modules:
  0.0 136.6 jit_solution(2786355192529247432)
XLA Ops:
  1.3 0.6 broadcast_in_dim.8.cnt_ref
  1.9 110.6 %shard_map.120 = (bf16[128,1024]{1,0:T(8,128)(2,1)}, bf16[2,384,1024]{2,1,0:T(8,128)(2,1)}, bf16[2,384,1024]{2,1,0:T(8,128)(2,1)}, bf16[14,384,256]{2,1,0:T(8,128)(2,1)}, bf16[14,384,512]{2,1,0:T(8,128)(2,1)}) custom-call(s32[8,128]{1,0:T(8,128)} %broadcast_in_dim.8.cnt_ref, bf16[128,1024]{1,0:T(8,128)(2,1)} %tok_ref.1, bf16[128,1024]{1,0:T(8,128)(2,1)} %cot_ref.1, ...), custom_call_target="tpu_custom_call" | custom-call | tf_op jit(solution)/shard_map/pallas_call | solution.py:454
  112.5 0.0 copy-start
  112.5 23.4 %shard_map.121 = (f32[1024,3584]{1,0:T(8,128)}, f32[1024,3584]{1,0:T(8,128)}, f32[3584,1024]{1,0:T(8,128)}) custom-call(s32[8,28]{1,0:T(8,128)} %gate_mask.3, s32[8,28]{1,0:T(8,128)} %up_mask.3, s32[8,28]{1,0:T(8,128)} %bitcast.4, bf16[2,384,1024]{2,1,0:T(8,128)(2,1)} %get-tuple-element.13.tokc, bf16[2,384,1024]{2,1,0:T(8,128)(2,1)} %get-tuple-element.14.gc, ...), custom_call_target="tpu_custom_call" | custom-call | tf_op jit(solution)/shard_map/pallas_call | solution.py:525
  135.9 0.0 copy-done
  135.9 0.7 copy.15
Async XLA Ops:
  112.5 23.5 %copy-start = (bf16[128,1024]{1,0:T(8,128)(2,1)S(1)}, bf16[128,1024]{1,0:T(8,128)(2,1)}, u32[]{:S(2)}) copy-start(bf16[128,1024]{1,0:T(8,128)(2,1)} %get-tuple-element.24) | copy-start | bytes 786436

commit v3 on v2

--- a/solution.py
+++ b/solution.py
@@ -25,6 +25,9 @@
         self.chunks = 2 * self.per_path
         k = self.levels
         self.bits = [list(range(k)), [0] + list(range(k - 1, 0, -1))]
+        first, dead = 16 * n_dp, n_col * tok_dev - self.rows
+        self.early = -(-(first + dead) // tok_dev) - 1
+        self.sections = [first, self.rows - first]
         self.orders = []
         for bits in self.bits:
             order = []
@@ -48,11 +51,11 @@
 def exchange_kernel(
     plan,
     cnt_ref, tok_ref, cot_ref, gate_mask, up_mask, down_mask, wg_hbm, wu_hbm, wd_hbm,
-    out_ref, tokc, gc, hid_out, d_out,
-    cnt_all, tok_all, cot_all, place, wg, wu, wd, w_sem,
-    keep, s0, r0, s1, r1, bkeep, bs0, br0, bs1, br1,
-    hid, dd, acc, zs, zr,
-    ring_sem, gu_sem, bk_sem, hid_sem, d_sem, z_sem, out_sem,
+    out_ref, tokc, d_out, down_out,
+    cnt_all, tok_all, cot_all, gc, place0, place1, tok0, tok1, wg, wu, wd, w_sem,
+    keep0, s00, r00, s10, r10, keep1, s01, r01, s11, r11, bkeep, bs0, br0, bs1, br1,
+    hid, dd, acc, zs, zr, down,
+    cnt_sem, ring_sem, gu0_sem, gu1_sem, bk_sem, hid_sem, d_sem, z_sem, out_sem, tok_sem,
 ):
     n_col, k, td, wide = plan.n_col, plan.levels, plan.tok_dev, plan.wide
     rows, piece, per, chunks = plan.rows, plan.piece, plan.per_path, plan.chunks
@@ -146,22 +149,26 @@
                 for copy in hop(bufs, way, step, "w"):
                     copy.wait_send()
 
-    tok_bufs = (0, [tok_all, cnt_all])
-    cot_bufs = (2, [cot_all])
+    def cnt_copy(step):
+        to = (col + step) % n_col
+        return remote(cnt_all.at[col], cnt_all.at[col], cnt_sem, (step - 1,), col=to)
+
+    for step in range(1, n_col):
+        cnt_copy(step).start()
+    tok_bufs = (0, [tok_all])
+    cot_bufs = (1, [cot_all])
     hop_start(tok_bufs, 0)
 
     side, parts = plan.feats // BLOCK, wide // BLOCK
 
-    def prune_in(lo, hi):
-        @pl.loop(lo, hi)
-        def _(u):
-            for copy in weight_copies(u)[:2]:
-                copy.wait()
-            for r in range(side):
-                for c in range(parts):
-                    at = (u, pl.ds(r * BLOCK, BLOCK), pl.ds(c * BLOCK, BLOCK))
-                    wg[at] = wg[at] * (gate_mask[r, u * parts + c] > 0).astype(F32).astype(BF16)
-                    wu[at] = wu[at] * (up_mask[r, u * parts + c] > 0).astype(F32).astype(BF16)
+    def prune_in(u):
+        for copy in weight_copies(u)[:2]:
+            copy.wait()
+        for r in range(side):
+            for c in range(parts):
+                at = (u, pl.ds(r * BLOCK, BLOCK), pl.ds(c * BLOCK, BLOCK))
+                wg[at] = wg[at] * (gate_mask[r, u * parts + c] > 0).astype(F32).astype(BF16)
+                wu[at] = wu[at] * (up_mask[r, u * parts + c] > 0).astype(F32).astype(BF16)
 
     def prune_down():
         @pl.loop(0, chunks)
@@ -172,54 +179,73 @@
                     at = (u, pl.ds(c * BLOCK, BLOCK), pl.ds(r * BLOCK, BLOCK))
                     wd[at] = wd[at] * (down_mask[r, u * parts + c] > 0).astype(F32).astype(BF16)
 
-    prune_in(0, per)
-    for step in range(1, n_col - 1):
-        hop_wait_recv(tok_bufs, step - 1)
-        hop_start(tok_bufs, step)
-        if step == 1:
-            prune_in(per, chunks)
-    hop_wait_recv(tok_bufs, n_col - 2)
-    hop_start(cot_bufs, 0)
-
-    lane = lax.broadcasted_iota(jnp.int32, (piece, td), 1)
-    row = lax.broadcasted_iota(jnp.int32, (piece, td), 0)
-    before = jnp.zeros((1, td), jnp.int32)
+    for step in range(1, n_col):
+        cnt_copy(step).wait_recv()
+
+    first, later = plan.sections
+    p0, p1 = first // plan.n_dp, later // plan.n_dp
+    counts = [cnt_all[shard][0:1, :] for shard in range(n_col)]
+
+    def far(shard):
+        return (shard - col) * (shard - col) * n_col + shard
+
     for shard in range(n_col):
-        count = cnt_all[shard][0:1, :]
+        count = counts[shard]
+        before = jnp.zeros((1, td), jnp.int32)
+        for other in range(n_col):
+            if other != shard:
+                nearer = (far(other) < far(shard)).astype(jnp.int32)
+                before = before + counts[other] * nearer
+        cols = slice(shard * td, (shard + 1) * td)
         for path in range(2):
             for i, owner in enumerate(plan.orders[path]):
                 target = 0
                 for bit in range(k):
                     mine = bit_of(dp, bit)
                     target = target + (1 - mine if owner >> bit & 1 else mine) * (1 << bit)
-                hit = (row + target * piece - before == lane) & (lane < count)
-                place[path, i * piece : (i + 1) * piece, shard * td : (shard + 1) * td] = jnp.where(
-                    hit, 1.0, 0.0
-                ).astype(BF16)
-        before = before + count
-
-    def compact(buf, to):
+                for into, size, base in ((place0, p0, 0), (place1, p1, first)):
+                    lane = lax.broadcasted_iota(jnp.int32, (size, td), 1)
+                    row = lax.broadcasted_iota(jnp.int32, (size, td), 0)
+                    hit = (row + (target * size + base) - before == lane) & (lane < count)
+                    ones = jnp.where(hit, 1.0, 0.0).astype(BF16)
+                    into[path, i * size : (i + 1) * size, cols] = ones
+
+    def compact(spots, buf):
         for path in range(2):
             total = None
             for shard in range(n_col):
                 part = jnp.dot(
-                    place[path, :, shard * td : (shard + 1) * td],
+                    spots[path, :, shard * td : (shard + 1) * td],
                     buf[shard],
                     preferred_element_type=F32,
                 )
                 total = part if total is None else total + part
-            to[path] = total.astype(BF16)
-
-    compact(tok_all, tokc)
+            yield path, total.astype(BF16)
+
+    def compact_early():
+        acc[...] = jnp.zeros_like(acc)
+        for shard in range(n_col):
+
+            @pl.when((shard - col <= plan.early) & (col - shard <= plan.early))
+            def _():
+                for path in range(2):
+                    acc[pl.ds(path * first, first)] += jnp.dot(
+                        place0[path, :, shard * td : (shard + 1) * td],
+                        tok_all[shard],
+                        preferred_element_type=F32,
+                    )
+
+        for path in range(2):
+            tok0[path] = acc[pl.ds(path * first, first)].astype(BF16)
 
     class Scatter:
-        def __init__(self, keep, s0, r0, s1, r1, sem):
-            self.keep, self.bufs, self.sem = keep, ((s0, r0), (s1, r1)), sem
+        def __init__(self, rows, keep, s0, r0, s1, r1, sem):
+            self.rows, self.keep, self.bufs, self.sem = rows, keep, ((s0, r0), (s1, r1)), sem
 
         def copy(self, path, level, u):
-            size = rows >> (level + 1)
+            size = self.rows >> (level + 1)
             src, dst = self.bufs[min(level, 1)]
-            start = 0 if level == 0 else (rows >> 1) - (rows >> level)
+            start = 0 if level == 0 else (self.rows >> 1) - (self.rows >> level)
             at = (u, pl.ds(start, size))
             return remote(
                 src.at[at], dst.at[at], self.sem, (level, u),
@@ -227,7 +253,7 @@
             )
 
         def put(self, path, u, value):
-            half = rows >> 1
+            half = self.rows >> 1
             src, _ = self.bufs[0]
             src[u] = value[half:].astype(BF16)
             self.keep[u] = value[:half]
@@ -236,22 +262,23 @@
         def got(self, path, level, u):
             copy = self.copy(path, level, u)
             copy.wait_recv()
-            size = rows >> (level + 1)
+            size = self.rows >> (level + 1)
             _, dst = self.bufs[min(level, 1)]
-            start = 0 if level == 0 else (rows >> 1) - (rows >> level)
+            start = 0 if level == 0 else (self.rows >> 1) - (self.rows >> level)
             return self.keep[u, 0:size] + dst[u, pl.ds(start, size)].astype(F32)
 
         def step(self, path, level, u):
             value = self.got(path, level - 1, u)
-            size = rows >> (level + 1)
-            start = (rows >> 1) - (rows >> level)
+            size = self.rows >> (level + 1)
+            start = (self.rows >> 1) - (self.rows >> level)
             src, _ = self.bufs[1]
             src[u, pl.ds(start, size)] = value[size:].astype(BF16)
             self.keep[u, 0:size] = value[:size]
             self.copy(path, level, u).start()
 
-    gu = Scatter(keep, s0, r0, s1, r1, gu_sem)
-    bk = Scatter(bkeep, bs0, br0, bs1, br1, bk_sem)
+    gu0 = Scatter(first, keep0, s00, r00, s10, r10, gu0_sem)
+    gu1 = Scatter(later, keep1, s01, r01, s11, r11, gu1_sem)
+    bk = Scatter(rows, bkeep, bs0, br0, bs1, br1, bk_sem)
 
     def gather_copy(buf, sem, path, level, u):
         size = rows >> (level + 1)
@@ -260,31 +287,81 @@
             dp=partner_of(dp, plan.bits[path][level]),
         )
 
-    def both(body):
-        for path in range(2):
-            body(path)
+    def gate_up(left, gu, u, path):
+        value = jnp.concatenate(
+            [
+                jnp.dot(left[path], wg[u], preferred_element_type=F32),
+                jnp.dot(left[path], wu[u], preferred_element_type=F32),
+            ],
+            axis=1,
+        )
+        gu.put(path, u, value)
+
+    def early_part(lo, hi):
+        @pl.loop(lo, hi)
+        def _(j):
+            for path in range(2):
+                u = path * per + j
+                prune_in(u)
+                gate_up(tok0, gu0, u, path)
+
+            @pl.when(j >= 1)
+            def _():
+                for path in range(2):
+                    gu0.step(path, 1, path * per + j - 1)
+
+    def hop_next(step):
+        hop_wait_recv(tok_bufs, step)
+        if step + 1 < n_col - 1:
+            hop_start(tok_bufs, step + 1)
+        else:
+            hop_start(cot_bufs, 0)
+
+    for step in range(plan.early):
+        hop_next(step)
+    compact_early()
+    early_part(0, per // 2)
+    if plan.early < n_col - 1:
+        hop_next(plan.early)
+    early_part(per // 2, per)
+    for step in range(plan.early + 1, n_col - 1):
+        hop_next(step)
+    for path in range(2):
+        gu0.step(path, 1, path * per + per - 1)
+    for path, value in compact(place1, tok_all):
+        tok1[path] = value
 
     @pl.loop(0, per)
     def _(j):
         for path in range(2):
-            u = path * per + j
-            left = tokc[path]
-            value = jnp.concatenate(
-                [
-                    jnp.dot(left, wg[u], preferred_element_type=F32),
-                    jnp.dot(left, wu[u], preferred_element_type=F32),
-                ],
-                axis=1,
-            )
-            gu.put(path, u, value)
+            gate_up(tok1, gu1, path * per + j, path)
 
         @pl.when(j >= 1)
         def _():
             for path in range(2):
-                gu.step(path, 1, path * per + j - 1)
+                gu1.step(path, 1, path * per + j - 1)
+
+        if k > 2:
+            for path in range(2):
+                gu0.step(path, 2, path * per + j)
 
     for path in range(2):
-        gu.step(path, 1, path * per + per - 1)
+        gu1.step(path, 1, path * per + per - 1)
+
+    def tok_copies(path, i):
+        return [
+            pltpu.make_async_copy(
+                src.at[path, pl.ds(i * size, size)],
+                tokc.at[path, pl.ds(i * piece + off, size)],
+                tok_sem.at[path, i, n],
+            )
+            for n, (src, size, off) in enumerate(((tok0, p0, 0), (tok1, p1, p0)))
+        ]
+
+    for path in range(2):
+        for i in range(plan.n_dp):
+            for copy in tok_copies(path, i):
+                copy.start()
 
     prune_down()
 
@@ -296,10 +373,14 @@
         @pl.loop(0, per)
         def _(j):
             for path in range(2):
-                gu.step(path, 2, path * per + j)
+                gu1.step(path, 2, path * per + j)
 
     hop_wait_recv(cot_bufs, n_col - 2)
-    compact(cot_all, gc)
+    for spots, size, off in ((place0, p0, 0), (place1, p1, p0)):
+        for path, value in compact(spots, cot_all):
+            for i in range(plan.n_dp):
+                at = i * piece + off
+                gc[path, at : at + size] = value[i * size : (i + 1) * size]
 
     @pl.loop(0, per)
     def _(j):
@@ -323,14 +404,17 @@
         @pl.loop(0, per)
         def _(j):
             for path in range(2):
-                gu.step(path, level, path * per + j)
+                gu0.step(path, level, path * per + j)
+                gu1.step(path, level, path * per + j)
 
     @pl.loop(0, per)
     def _(j):
         for path in range(2):
             u = path * per + j
-            value = gu.got(path, k - 1, u)
-            keep[u, 0:piece] = value
+            value0, value1 = gu0.got(path, k - 1, u), gu1.got(path, k - 1, u)
+            keep0[u, 0:p0] = value0
+            keep1[u, 0:p1] = value1
+            value = jnp.concatenate([value0, value1], axis=0)
             gate, upward = value[:, :wide], value[:, wide:]
             sigma = 1.0 / (1.0 + jnp.exp(-gate))
             hid[u, 0:piece] = (gate * sigma * upward).astype(BF16)
@@ -361,7 +445,8 @@
         for path in range(2):
             u = path * per + j
             back = bk.got(path, k - 1, u)
-            gate, upward = keep[u, 0:piece, 0:wide], keep[u, 0:piece, wide : 2 * wide]
+            value = jnp.concatenate([keep0[u, 0:p0], keep1[u, 0:p1]], axis=0)
+            gate, upward = value[:, :wide], value[:, wide:]
             sigma = 1.0 / (1.0 + jnp.exp(-gate))
             dd[u, 0:piece, 0:wide] = (
                 back * upward * sigma * (1.0 + gate * (1.0 - sigma))
@@ -376,21 +461,28 @@
         for path in range(2):
             u = path * per + j
             gather_copy(hid, hid_sem, path, 0, u).wait_recv()
-            pltpu.make_async_copy(hid.at[u], hid_out.at[u], out_sem.at[0, u]).start()
-            acc[path] += jnp.dot(hid[u], wd[u], preferred_element_type=F32)
-
-    for i, owner in enumerate(plan.orders[0]):
-        other = plan.orders[1].index(owner)
-        at = pl.ds(i * piece, piece)
-        acc[0, at] = acc[0, at] + acc[1, pl.ds(other * piece, piece)]
-    mixed = acc[0].astype(BF16)
+            left = hid[u]
+            if path == 1:
+                spots = [plan.orders[1].index(owner) * piece for owner in plan.orders[0]]
+                left = jnp.concatenate([left[at : at + piece] for at in spots], axis=0)
+            acc[0:rows] += jnp.dot(left, wd[u], preferred_element_type=F32)
+
+    mixed = acc[0:rows].astype(BF16)
+    mixes = [
+        jnp.concatenate([mixed[at : at + size] for at in range(off, rows, piece)], axis=0)
+        for size, off in ((p0, 0), (p1, p0))
+    ]
     for shard in range(n_col):
-        zs[shard] = lax.dot_general(
-            place[0, :, shard * td : (shard + 1) * td],
-            mixed,
-            (((0,), (0,)), ((), ())),
-            preferred_element_type=F32,
-        ).astype(BF16)
+        total = None
+        for spots, mix in zip((place0, place1), mixes):
+            part = lax.dot_general(
+                spots[0, :, shard * td : (shard + 1) * td],
+                mix,
+                (((0,), (0,)), ((), ())),
+                preferred_element_type=F32,
+            )
+            total = part if total is None else total + part
+        zs[shard] = total.astype(BF16)
 
     def z_copy(step):
         to = (col + step) % n_col
@@ -399,7 +491,30 @@
     for step in range(1, n_col):
         z_copy(step).start()
 
-    for level in range(k - 2, -1, -1):
+    gather_step(dd, d_sem, k - 2)
+
+    def down_copy(path, u):
+        return pltpu.make_async_copy(
+            down.at[path],
+            down_out.at[pl.ds(pl.multiple_of(u * wide, wide), wide), :],
+            out_sem.at[0, path],
+        )
+
+    @pl.loop(0, per)
+    def _(j):
+        for path in range(2):
+            u = path * per + j
+
+            @pl.when(j >= 1)
+            def _():
+                down_copy(path, u - 1).wait()
+
+            down[path] = lax.dot_general(
+                hid[u], gc[path], (((0,), (0,)), ((), ())), preferred_element_type=F32
+            ).astype(BF16)
+            down_copy(path, u).start()
+
+    for level in range(k - 3, -1, -1):
         gather_step(dd, d_sem, level)
 
     @pl.loop(0, per)
@@ -418,31 +533,39 @@
     for step in range(1, n_col):
         z_copy(step).wait_send()
     for step in range(n_col - 1):
+        cnt_copy(step + 1).wait_send()
         hop_wait_send(tok_bufs, step)
         hop_wait_send(cot_bufs, step)
 
+    for path in range(2):
+        down_copy(path, path * per + per - 1).wait()
+        for i in range(plan.n_dp):
+            for copy in tok_copies(path, i):
+                copy.wait()
+
     @pl.loop(0, per)
     def _(j):
         for path in range(2):
             u = path * per + j
             for level in range(k):
-                gu.copy(path, level, u).wait_send()
+                gu0.copy(path, level, u).wait_send()
+                gu1.copy(path, level, u).wait_send()
                 bk.copy(path, level, u).wait_send()
                 gather_copy(hid, hid_sem, path, level, u).wait_send()
                 gather_copy(dd, d_sem, path, level, u).wait_send()
-            pltpu.make_async_copy(hid.at[u], hid_out.at[u], out_sem.at[0, u]).wait()
             pltpu.make_async_copy(dd.at[u], d_out.at[u], out_sem.at[1, u]).wait()
 
 
 def exchange(plan, cnt, tokens, cotangent, gate_mask, up_mask, down_mask, wg, wu, wd):
     n_col, k, td, wide = plan.n_col, plan.levels, plan.tok_dev, plan.wide
     rows, chunks, feats = plan.rows, plan.chunks, plan.feats
+    first, later = plan.sections
     vmem, smem = pl.BlockSpec(memory_space=pltpu.VMEM), pl.BlockSpec(memory_space=pltpu.SMEM)
     whole = pl.BlockSpec(memory_space=pl.ANY)
-    half = rows // 2
-    rest = half - (rows >> k)
-
-    def scatter_bufs(width):
+
+    def scatter_bufs(rows, width):
+        half = rows // 2
+        rest = half - (rows >> k)
         return [
             pltpu.VMEM((chunks, half, width), F32),
             pltpu.VMEM((chunks, half, width), BF16),
@@ -456,35 +579,43 @@
         out_shape=(
             jax.ShapeDtypeStruct((td, feats), BF16),
             jax.ShapeDtypeStruct((2, rows, feats), BF16),
-            jax.ShapeDtypeStruct((2, rows, feats), BF16),
-            jax.ShapeDtypeStruct((chunks, rows, wide), BF16),
             jax.ShapeDtypeStruct((chunks, rows, 2 * wide), BF16),
+            jax.ShapeDtypeStruct((plan.units, feats), BF16),
         ),
         in_specs=[vmem, vmem, vmem, smem, smem, smem, whole, whole, whole],
-        out_specs=(vmem, vmem, vmem, whole, whole),
+        out_specs=(vmem, whole, whole, whole),
         scratch_shapes=[
             pltpu.VMEM((n_col, 8, 128), jnp.int32),
             pltpu.VMEM((n_col, td, feats), BF16),
             pltpu.VMEM((n_col, td, feats), BF16),
-            pltpu.VMEM((2, rows, n_col * td), BF16),
+            pltpu.VMEM((2, rows, feats), BF16),
+            pltpu.VMEM((2, first, n_col * td), BF16),
+            pltpu.VMEM((2, later, n_col * td), BF16),
+            pltpu.VMEM((2, first, feats), BF16),
+            pltpu.VMEM((2, later, feats), BF16),
             pltpu.VMEM((chunks, feats, wide), BF16),
             pltpu.VMEM((chunks, feats, wide), BF16),
             pltpu.VMEM((chunks, wide, feats), BF16),
             pltpu.SemaphoreType.DMA((3, chunks)),
-            *scatter_bufs(2 * wide),
-            *scatter_bufs(wide),
+            *scatter_bufs(first, 2 * wide),
+            *scatter_bufs(later, 2 * wide),
+            *scatter_bufs(rows, wide),
             pltpu.VMEM((chunks, rows, wide), BF16),
             pltpu.VMEM((chunks, rows, 2 * wide), BF16),
-            pltpu.VMEM((2, rows, feats), F32),
+            pltpu.VMEM((max(rows, 2 * first), feats), F32),
             pltpu.VMEM((n_col, td, feats), BF16),
             pltpu.VMEM((n_col - 1, td, feats), BF16),
-            pltpu.SemaphoreType.DMA((2, 3, 2, n_col - 1)),
+            pltpu.VMEM((2, wide, feats), BF16),
+            pltpu.SemaphoreType.DMA((2, n_col - 1)),
+            pltpu.SemaphoreType.DMA((2, 2, 2, n_col - 1)),
+            pltpu.SemaphoreType.DMA((2, k, chunks)),
             pltpu.SemaphoreType.DMA((2, k, chunks)),
             pltpu.SemaphoreType.DMA((2, k, chunks)),
             pltpu.SemaphoreType.DMA((2, k, chunks)),
             pltpu.SemaphoreType.DMA((2, k, chunks)),
             pltpu.SemaphoreType.DMA((2, n_col - 1)),
             pltpu.SemaphoreType.DMA((2, chunks)),
+            pltpu.SemaphoreType.DMA((2, plan.n_dp, 2)),
         ],
         compiler_params=pltpu.CompilerParams(
             collective_id=0, has_side_effects=True, vmem_limit_bytes=63 * 2**20
@@ -493,7 +624,7 @@
 
 
 def grads_kernel(
-    plan, gate_mask, up_mask, down_mask, tokc, gc, hid, dd, gate_grad, up_grad, down_grad, turned
+    plan, gate_mask, up_mask, down_mask, tokc, dd, down, gate_grad, up_grad, down_grad, turned
 ):
     u = pl.program_id(0)
     wide = plan.wide
@@ -512,14 +643,13 @@
             for c in range(parts):
                 rs, cs = slice(r * BLOCK, (r + 1) * BLOCK), slice(c * BLOCK, (c + 1) * BLOCK)
                 ref[rs, cs] = keep(mask[r, u * parts + c], value[rs, cs])
-    value = jnp.dot(hid[0].T, gc[0], preferred_element_type=F32)
     for r in range(side):
         for c in range(parts):
             rs, cs = slice(r * BLOCK, (r + 1) * BLOCK), slice(c * BLOCK, (c + 1) * BLOCK)
-            down_grad[cs, rs] = keep(down_mask[r, u * parts + c], value[cs, rs])
-
-
-def grads(plan, gate_mask, up_mask, down_mask, tokc, gc, hid, dd):
+            down_grad[cs, rs] = keep(down_mask[r, u * parts + c], down[cs, rs].astype(F32))
+
+
+def grads(plan, gate_mask, up_mask, down_mask, tokc, dd, down):
     rows, feats, wide, per = plan.rows, plan.feats, plan.wide, plan.per_path
     smem = pl.BlockSpec(memory_space=pltpu.SMEM)
     return pl.pallas_call(
@@ -535,9 +665,8 @@
             smem,
             smem,
             pl.BlockSpec((1, rows, feats), lambda u: (u // per, 0, 0)),
-            pl.BlockSpec((1, rows, feats), lambda u: (u // per, 0, 0)),
-            pl.BlockSpec((1, rows, wide), lambda u: (u, 0, 0)),
             pl.BlockSpec((1, rows, 2 * wide), lambda u: (u, 0, 0)),
+            pl.BlockSpec((wide, feats), lambda u: (u, 0)),
         ],
         out_specs=(
             pl.BlockSpec((feats, wide), lambda u: (0, u)),
@@ -546,7 +675,7 @@
         ),
         scratch_shapes=[pltpu.VMEM((feats, rows), BF16)],
         compiler_params=pltpu.CompilerParams(vmem_limit_bytes=63 * 2**20),
-    )(gate_mask, up_mask, down_mask, tokc, gc, hid, dd)
+    )(gate_mask, up_mask, down_mask, tokc, dd, down)
 
 
 def on_device(
@@ -556,11 +685,11 @@
     plan = Plan(n_col, n_dp, tokens.shape[0], tokens.shape[1], gate_weight.shape[1])
     cnt = jnp.broadcast_to(counts.reshape(1, 1), (8, 128))
     down_mask = down_mask.T
-    output, tokc, gc, hid, dd = exchange(
+    output, tokc, dd, down = exchange(
         plan, cnt, tokens, cotangent, gate_mask, up_mask, down_mask,
         gate_weight, up_weight, down_weight,
     )
-    gate_grad, up_grad, down_grad = grads(plan, gate_mask, up_mask, down_mask, tokc, gc, hid, dd)
+    gate_grad, up_grad, down_grad = grads(plan, gate_mask, up_mask, down_mask, tokc, dd, down)
     return (output, gate_grad, up_grad, down_grad)
 
 

time: 137 us -> 138 us (level)
    pallas_call x1, Pallas kernels: 111 us -> 112 us  [exchange(): pl.pallas_call(functools.partial(exchange_kernel, plan), out_shape=(jax.S...]
where the time goes in v3:
time: 138 us
  Pallas kernels  135 us (98%)
    pallas_call x1, Pallas kernels, exchange(): pl.pallas_call(functools.partial(exchange_kernel, plan), out_shape=(jax.S...  112 us
    pallas_call x1, Pallas kernels, grads(): pl.pallas_call(functools.partial(grads_kernel, plan), grid=(plan.chunks,)...  23.2 us

profile of v3, /device:TPU:0, one launch (start us, length us, event | category | flops | bytes accessed | tf_op | source)
XLA Modules:
  0.0 137.9 jit_solution(13260531544265734457)
XLA Ops:
  1.3 0.6 broadcast_in_dim.8.cnt_ref
  1.9 112.1 %shard_map.120 = (bf16[128,1024]{1,0:T(8,128)(2,1)}, bf16[2,384,1024]{2,1,0:T(8,128)(2,1)}, bf16[14,384,512]{2,1,0:T(8,128)(2,1)}, bf16[3584,1024]{1,0:T(8,128)(2,1)}) custom-call(s32[8,128]{1,0:T(8,128)} %broadcast_in_dim.8.cnt_ref, bf16[128,1024]{1,0:T(8,128)(2,1)} %tok_ref.1, bf16[128,1024]{1,0:T(8,128)(2,1)} %cot_ref.1, s32[8,28]{1,0:T(8,128)} %gate_mask.3, ...), custom_call_target="tpu_custom_call" | custom-call | tf_op jit(solution)/shard_map/pallas_call | solution.py:577
  114.0 0.0 copy-start
  114.0 23.2 %shard_map.121 = (f32[1024,3584]{1,0:T(8,128)}, f32[1024,3584]{1,0:T(8,128)}, f32[3584,1024]{1,0:T(8,128)}) custom-call(s32[8,28]{1,0:T(8,128)} %gate_mask.3, s32[8,28]{1,0:T(8,128)} %up_mask.3, s32[8,28]{1,0:T(8,128)} %bitcast.4, bf16[2,384,1024]{2,1,0:T(8,128)(2,1)} %get-tuple-element.12.tokc, bf16[14,384,512]{2,1,0:T(8,128)(2,1)} %get-tuple-element.13.dd, ...), custom_call_target="tpu_custom_call" | custom-call | tf_op jit(solution)/shard_map/pallas_call | solution.py:655
  137.2 0.0 copy-done
  137.2 0.7 copy.15
Async XLA Ops:
  114.0 23.2 %copy-start = (bf16[128,1024]{1,0:T(8,128)(2,1)S(1)}, bf16[128,1024]{1,0:T(8,128)(2,1)}, u32[]{:S(2)}) copy-start(bf16[128,1024]{1,0:T(8,128)(2,1)} %get-tuple-element.22) | copy-start | bytes 786436

commit v4 on v3

--- a/solution.py
+++ b/solution.py
@@ -51,10 +51,10 @@
 def exchange_kernel(
     plan,
     cnt_ref, tok_ref, cot_ref, gate_mask, up_mask, down_mask, wg_hbm, wu_hbm, wd_hbm,
-    out_ref, tokc, d_out, down_out,
-    cnt_all, tok_all, cot_all, gc, place0, place1, tok0, tok1, wg, wu, wd, w_sem,
+    out_ref, tokc, gc, hid_out, d_out,
+    cnt_all, tok_all, cot_all, place0, place1, tok0, tok1, wg, wu, wd, w_sem,
     keep0, s00, r00, s10, r10, keep1, s01, r01, s11, r11, bkeep, bs0, br0, bs1, br1,
-    hid, dd, acc, zs, zr, down,
+    hid, dd, acc, zs, zr,
     cnt_sem, ring_sem, gu0_sem, gu1_sem, bk_sem, hid_sem, d_sem, z_sem, out_sem, tok_sem,
 ):
     n_col, k, td, wide = plan.n_col, plan.levels, plan.tok_dev, plan.wide
@@ -460,7 +460,10 @@
     def _(j):
         for path in range(2):
             u = path * per + j
+            gather_copy(dd, d_sem, path, k - 1, u).wait_recv()
+            gather_copy(dd, d_sem, path, k - 2, u).start()
             gather_copy(hid, hid_sem, path, 0, u).wait_recv()
+            pltpu.make_async_copy(hid.at[u], hid_out.at[u], out_sem.at[0, u]).start()
             left = hid[u]
             if path == 1:
                 spots = [plan.orders[1].index(owner) * piece for owner in plan.orders[0]]
@@ -491,29 +494,6 @@
     for step in range(1, n_col):
         z_copy(step).start()
 
-    gather_step(dd, d_sem, k - 2)
-
-    def down_copy(path, u):
-        return pltpu.make_async_copy(
-            down.at[path],
-            down_out.at[pl.ds(pl.multiple_of(u * wide, wide), wide), :],
-            out_sem.at[0, path],
-        )
-
-    @pl.loop(0, per)
-    def _(j):
-        for path in range(2):
-            u = path * per + j
-
-            @pl.when(j >= 1)
-            def _():
-                down_copy(path, u - 1).wait()
-
-            down[path] = lax.dot_general(
-                hid[u], gc[path], (((0,), (0,)), ((), ())), preferred_element_type=F32
-            ).astype(BF16)
-            down_copy(path, u).start()
-
     for level in range(k - 3, -1, -1):
         gather_step(dd, d_sem, level)
 
@@ -538,7 +518,6 @@
         hop_wait_send(cot_bufs, step)
 
     for path in range(2):
-        down_copy(path, path * per + per - 1).wait()
         for i in range(plan.n_dp):
             for copy in tok_copies(path, i):
                 copy.wait()
@@ -553,6 +532,7 @@
                 bk.copy(path, level, u).wait_send()
                 gather_copy(hid, hid_sem, path, level, u).wait_send()
                 gather_copy(dd, d_sem, path, level, u).wait_send()
+            pltpu.make_async_copy(hid.at[u], hid_out.at[u], out_sem.at[0, u]).wait()
             pltpu.make_async_copy(dd.at[u], d_out.at[u], out_sem.at[1, u]).wait()
 
 
@@ -579,16 +559,16 @@
         out_shape=(
             jax.ShapeDtypeStruct((td, feats), BF16),
             jax.ShapeDtypeStruct((2, rows, feats), BF16),
+            jax.ShapeDtypeStruct((2, rows, feats), BF16),
+            jax.ShapeDtypeStruct((chunks, rows, wide), BF16),
             jax.ShapeDtypeStruct((chunks, rows, 2 * wide), BF16),
-            jax.ShapeDtypeStruct((plan.units, feats), BF16),
         ),
         in_specs=[vmem, vmem, vmem, smem, smem, smem, whole, whole, whole],
-        out_specs=(vmem, whole, whole, whole),
+        out_specs=(vmem, whole, vmem, whole, whole),
         scratch_shapes=[
             pltpu.VMEM((n_col, 8, 128), jnp.int32),
             pltpu.VMEM((n_col, td, feats), BF16),
             pltpu.VMEM((n_col, td, feats), BF16),
-            pltpu.VMEM((2, rows, feats), BF16),
             pltpu.VMEM((2, first, n_col * td), BF16),
             pltpu.VMEM((2, later, n_col * td), BF16),
             pltpu.VMEM((2, first, feats), BF16),
@@ -605,7 +585,6 @@
             pltpu.VMEM((max(rows, 2 * first), feats), F32),
             pltpu.VMEM((n_col, td, feats), BF16),
             pltpu.VMEM((n_col - 1, td, feats), BF16),
-            pltpu.VMEM((2, wide, feats), BF16),
             pltpu.SemaphoreType.DMA((2, n_col - 1)),
             pltpu.SemaphoreType.DMA((2, 2, 2, n_col - 1)),
             pltpu.SemaphoreType.DMA((2, k, chunks)),
@@ -624,7 +603,7 @@
 
 
 def grads_kernel(
-    plan, gate_mask, up_mask, down_mask, tokc, dd, down, gate_grad, up_grad, down_grad, turned
+    plan, gate_mask, up_mask, down_mask, tokc, gc, hid, dd, gate_grad, up_grad, down_grad, turned
 ):
     u = pl.program_id(0)
     wide = plan.wide
@@ -643,13 +622,14 @@
             for c in range(parts):
                 rs, cs = slice(r * BLOCK, (r + 1) * BLOCK), slice(c * BLOCK, (c + 1) * BLOCK)
                 ref[rs, cs] = keep(mask[r, u * parts + c], value[rs, cs])
+    value = jnp.dot(hid[0].T, gc[0], preferred_element_type=F32)
     for r in range(side):
         for c in range(parts):
             rs, cs = slice(r * BLOCK, (r + 1) * BLOCK), slice(c * BLOCK, (c + 1) * BLOCK)
-            down_grad[cs, rs] = keep(down_mask[r, u * parts + c], down[cs, rs].astype(F32))
-
-
-def grads(plan, gate_mask, up_mask, down_mask, tokc, dd, down):
+            down_grad[cs, rs] = keep(down_mask[r, u * parts + c], value[cs, rs])
+
+
+def grads(plan, gate_mask, up_mask, down_mask, tokc, gc, hid, dd):
     rows, feats, wide, per = plan.rows, plan.feats, plan.wide, plan.per_path
     smem = pl.BlockSpec(memory_space=pltpu.SMEM)
     return pl.pallas_call(
@@ -665,8 +645,9 @@
             smem,
             smem,
             pl.BlockSpec((1, rows, feats), lambda u: (u // per, 0, 0)),
+            pl.BlockSpec((1, rows, feats), lambda u: (u // per, 0, 0)),
+            pl.BlockSpec((1, rows, wide), lambda u: (u, 0, 0)),
             pl.BlockSpec((1, rows, 2 * wide), lambda u: (u, 0, 0)),
-            pl.BlockSpec((wide, feats), lambda u: (u, 0)),
         ],
         out_specs=(
             pl.BlockSpec((feats, wide), lambda u: (0, u)),
@@ -675,7 +656,7 @@
         ),
         scratch_shapes=[pltpu.VMEM((feats, rows), BF16)],
         compiler_params=pltpu.CompilerParams(vmem_limit_bytes=63 * 2**20),
-    )(gate_mask, up_mask, down_mask, tokc, dd, down)
+    )(gate_mask, up_mask, down_mask, tokc, gc, hid, dd)
 
 
 def on_device(
@@ -685,11 +666,11 @@
     plan = Plan(n_col, n_dp, tokens.shape[0], tokens.shape[1], gate_weight.shape[1])
     cnt = jnp.broadcast_to(counts.reshape(1, 1), (8, 128))
     down_mask = down_mask.T
-    output, tokc, dd, down = exchange(
+    output, tokc, gc, hid, dd = exchange(
         plan, cnt, tokens, cotangent, gate_mask, up_mask, down_mask,
         gate_weight, up_weight, down_weight,
     )
-    gate_grad, up_grad, down_grad = grads(plan, gate_mask, up_mask, down_mask, tokc, dd, down)
+    gate_grad, up_grad, down_grad = grads(plan, gate_mask, up_mask, down_mask, tokc, gc, hid, dd)
     return (output, gate_grad, up_grad, down_grad)
 
 

time: 138 us -> 141 us (1.022)
  Pallas kernels: 135 us -> 138 us
    pallas_call x1, Pallas kernels: 112 us -> 114 us  [exchange(): pl.pallas_call(functools.partial(exchange_kernel, plan), out_shape=(jax.S...]
where the time goes in v4:
time: 141 us; the launch traced here: 140 us
  Pallas kernels  138 us (98%)
    pallas_call x1, Pallas kernels, exchange(): pl.pallas_call(functools.partial(exchange_kernel, plan), out_shape=(jax.S...  114 us
    pallas_call x1, Pallas kernels, grads(): pl.pallas_call(functools.partial(grads_kernel, plan), grid=(plan.chunks,)...  23.4 us

profile of v4, /device:TPU:0, one launch (start us, length us, event | category | flops | bytes accessed | tf_op | source)
XLA Modules:
  0.0 140.3 jit_solution(12497178306036587974)
XLA Ops:
  1.3 0.6 broadcast_in_dim.8.cnt_ref
  1.9 114.3 %shard_map.120 = (bf16[128,1024]{1,0:T(8,128)(2,1)}, bf16[2,384,1024]{2,1,0:T(8,128)(2,1)}, bf16[2,384,1024]{2,1,0:T(8,128)(2,1)}, bf16[14,384,256]{2,1,0:T(8,128)(2,1)}, bf16[14,384,512]{2,1,0:T(8,128)(2,1)}) custom-call(s32[8,128]{1,0:T(8,128)} %broadcast_in_dim.8.cnt_ref, bf16[128,1024]{1,0:T(8,128)(2,1)} %tok_ref.1, bf16[128,1024]{1,0:T(8,128)(2,1)} %cot_ref.1, ...), custom_call_target="tpu_custom_call" | custom-call | tf_op jit(solution)/shard_map/pallas_call | solution.py:557
  116.1 0.0 copy-start
  116.2 23.4 %shard_map.121 = (f32[1024,3584]{1,0:T(8,128)}, f32[1024,3584]{1,0:T(8,128)}, f32[3584,1024]{1,0:T(8,128)}) custom-call(s32[8,28]{1,0:T(8,128)} %gate_mask.3, s32[8,28]{1,0:T(8,128)} %up_mask.3, s32[8,28]{1,0:T(8,128)} %bitcast.4, bf16[2,384,1024]{2,1,0:T(8,128)(2,1)} %get-tuple-element.13.tokc, bf16[2,384,1024]{2,1,0:T(8,128)(2,1)} %get-tuple-element.14.gc, ...), custom_call_target="tpu_custom_call" | custom-call | tf_op jit(solution)/shard_map/pallas_call | solution.py:635
  139.6 0.0 copy-done
  139.6 0.7 copy.15
Async XLA Ops:
  116.1 23.4 %copy-start = (bf16[128,1024]{1,0:T(8,128)(2,1)S(1)}, bf16[128,1024]{1,0:T(8,128)(2,1)}, u32[]{:S(2)}) copy-start(bf16[128,1024]{1,0:T(8,128)(2,1)} %get-tuple-element.24) | copy-start | bytes 786436
